TPU v7x, 32 devices: a whole 2x2x4 slice. The times are simulated.
32 devices in a mesh: groups: 2 (over y), dp: 4 (over z), tensor: 4 (over x, core).
Axes of the slice: x: 2, y: 2, z: 4, core: 2. Of those that a mesh axis runs over, the one named last changes fastest.
Arguments:
- patches: bfloat16 [8192, 1280], P(('groups', 'dp')), parts along dimension 0, may hold values from -64 to 64
- grids: int32 [8, 2], P(('groups', 'dp')), parts along dimension 0, may hold values from 16 to 32, as said below
- dest: int32 [8, 256], P(('groups', 'dp')), parts along dimension 0, may hold values from 0 to 1535, as said below
- norm_gain: float32 [1280], replicated, may hold values from 0.1 to 1.9
- qkv_weight: bfloat16 [3, 1280, 1280], P(None, None, 'tensor'), may hold values from -8 to 8
- qkv_bias: float32 [3, 1280], P(None, 'tensor'), may hold values from -3 to 3
- proj_weight: bfloat16 [1280, 1280], P('tensor'), may hold values from -0.15625 to 0.15625
- proj_bias: float32 [1280], replicated, may hold values from -3 to 3
- merge_gain: float32 [1280], replicated, may hold values from 0.1 to 1.9
- w_first: bfloat16 [5120, 5120], P('dp', 'tensor'), may hold values from -0.078125 to 0.078125
- b_first: float32 [5120], P('tensor'), may hold values from -3 to 3
- w_second: bfloat16 [5120, 8192], P('tensor', 'dp'), may hold values from -0.078125 to 0.078125
- b_second: float32 [8192], P('tensor'), may hold values from -3 to 3
- text_embed: bfloat16 [3072, 8192], P(('groups', 'dp'), 'tensor'), parts along dimension 0, may hold values from -6 to 6
Outputs:
- sequence: bfloat16 [3072, 8192], P(('groups', 'dp'), 'tensor'), parts along dimension 0
There are 2 independent parts, one for each index of `groups`. A program takes and returns all parts, laid end to end along the dimension named above; an argument that names none is the same for every part. Nothing has to cross between parts.
Inputs may be any that keep to these rules, and one draw needn't show every extreme that they name: `grids`: both sides of every grid are even, at least 16 and at most 32; in each part along `groups`, the first image (the one on dp index 0) has the full 32 x 32 grid. The rows dest[i, j] with j < grids[i, 0] * grids[i, 1] / 4 are distinct over all images; the live rows of one image reach at most 64 rows in each aligned block of 384 sequence rows, and exactly that many for a full grid.
All inputs are finite; a program needn't handle non-finite values.
Results may differ from a plain program's by a relative error of at most 0.014.
Values may be sent and summed in bfloat16 or wider, within the bound.
No kernel may reach another device: no remote copies, remote signals or barrier semaphores. Data moves between devices by JAX's collectives and lax.ppermute only.
A program may use at most 128 MiB of HBM per device.

v0:
```python
import math

import jax
import jax.numpy as jnp
from jax import lax
from jax.sharding import PartitionSpec as P

HEAD_DIM = 80
PATCHES = 1024
MERGED = 256


def rms_scale(values, gain):
    return values * lax.rsqrt(jnp.mean(values * values, axis=-1, keepdims=True) + 1e-06) * gain


def local(
    patches,
    grids,
    dest,
    norm_gain,
    qkv_weight,
    qkv_bias,
    proj_weight,
    proj_bias,
    merge_gain,
    w_first,
    b_first,
    w_second,
    b_second,
    text_embed,
):
    rows_dev = patches.shape[0]
    images_dev = grids.shape[0]
    heads_dev = qkv_weight.shape[2] // HEAD_DIM
    live_count = grids[:, 0] * grids[:, 1]
    normed = rms_scale(patches.astype(jnp.float32), norm_gain).astype(jnp.bfloat16)
    projected = (
        jnp.einsum("rv,jvc->jrc", normed, qkv_weight, preferred_element_type=jnp.float32)
        + qkv_bias[:, None, :]
    )
    projected = projected.astype(jnp.bfloat16).reshape(3, images_dev, PATCHES, heads_dev, HEAD_DIM)
    scores = jnp.einsum(
        "iqhd,ikhd->ihqk", projected[0], projected[1], preferred_element_type=jnp.float32
    ) / math.sqrt(HEAD_DIM)
    live_keys = jnp.arange(PATCHES, dtype=jnp.int32)[None, :] < live_count[:, None]
    scores = jnp.where(live_keys[:, None, None, :], scores, jnp.float32(-1e30))
    peak_score = jnp.max(scores, axis=-1, keepdims=True)
    exponent = jnp.exp(scores - peak_score)
    weights = (exponent / jnp.sum(exponent, axis=-1, keepdims=True)).astype(jnp.bfloat16)
    attended = jnp.einsum(
        "ihqk,ikhd->iqhd", weights, projected[2], preferred_element_type=jnp.float32
    )
    attended = attended.astype(jnp.bfloat16).reshape(rows_dev, heads_dev * HEAD_DIM)
    partial_value = jnp.dot(attended, proj_weight, preferred_element_type=jnp.float32).astype(
        jnp.bfloat16
    )
    summed = lax.psum(partial_value, "tensor").astype(jnp.float32)
    resid = patches.astype(jnp.float32) + summed + proj_bias
    merged_in = rms_scale(resid, merge_gain).astype(jnp.bfloat16)
    merged_in = merged_in.reshape(rows_dev // 4, 4 * patches.shape[1])
    merged_dev = merged_in.shape[0]
    received = lax.all_to_all(merged_in, "dp", split_axis=1, concat_axis=0, tiled=True)
    first_out = lax.psum_scatter(
        jnp.dot(received, w_first, preferred_element_type=jnp.float32).astype(jnp.bfloat16),
        "dp",
        scatter_dimension=0,
        tiled=True,
    ).astype(jnp.float32)
    hidden = jax.nn.gelu(first_out + b_first, approximate=False).astype(jnp.bfloat16)
    second_rows = jnp.dot(
        hidden,
        lax.all_gather(w_second, "dp", axis=1, tiled=True),
        preferred_element_type=jnp.float32,
    ).astype(jnp.bfloat16)
    visual = lax.psum_scatter(second_rows, "tensor", scatter_dimension=1, tiled=True).astype(
        jnp.float32
    )
    visual = (visual + b_second).astype(jnp.bfloat16)
    feature_count = visual.shape[1]
    dp_count = lax.axis_size("dp")
    seq_rows = text_embed.shape[0]
    capacity = images_dev * (MERGED // dp_count)
    live_rows = (jnp.arange(MERGED, dtype=jnp.int32)[None, :] < (live_count // 4)[:, None]).reshape(
        merged_dev
    )
    dest_flat = dest.reshape(merged_dev)
    shard_id = jnp.where(live_rows, dest_flat // seq_rows, dp_count)
    local_row = dest_flat % seq_rows
    one_hot = (shard_id[:, None] == jnp.arange(dp_count, dtype=jnp.int32)[None, :]).astype(
        jnp.int32
    )
    before = jnp.cumsum(one_hot, axis=0) - one_hot
    slot_index = jnp.sum(before * one_hot, axis=1)
    buffer = (
        jnp.zeros((dp_count, capacity, feature_count), jnp.bfloat16)
        .at[shard_id, slot_index]
        .set(visual, mode="drop")
    )
    positions = (
        jnp.full((dp_count, capacity), seq_rows, jnp.int32)
        .at[shard_id, slot_index]
        .set(local_row, mode="drop")
    )
    arrived, arrived_rows = (
        lax.all_to_all(buffer, "dp", split_axis=0, concat_axis=0, tiled=True),
        lax.all_to_all(positions, "dp", split_axis=0, concat_axis=0, tiled=True),
    )
    sequence = text_embed.at[arrived_rows.reshape(-1)].set(
        arrived.reshape(-1, feature_count), mode="drop"
    )
    return sequence


def solution(mesh):
    in_specs = (
        P(("groups", "dp"), None),
        P(("groups", "dp"), None),
        P(("groups", "dp"), None),
        P(),
        P(None, None, "tensor"),
        P(None, "tensor"),
        P("tensor", None),
        P(),
        P(),
        P("dp", "tensor"),
        P("tensor"),
        P("tensor", "dp"),
        P("tensor"),
        P(("groups", "dp"), "tensor"),
    )
    out_specs = P(("groups", "dp"), "tensor")
    return jax.shard_map(local, mesh=mesh, in_specs=in_specs, out_specs=out_specs, check_vma=False)
```

profile of v0, /device:TPU:0, one launch (start us, length us, event | category | flops | bytes accessed | tf_op | source)
XLA Modules:
  0.0 749.2 jit_solution(11529100986900097305)
XLA Ops:
  6.5 2.9 copy.35
  13.1 2.8 fusion.15
  15.9 1.3 fusion.103
  17.3 10.9 %fusion.105 = (f32[4,1024]{1,0:T(4,128)S(1)}, f32[4,1024,1024]{1,2,0:T(8,128)}) fusion(pred[1024]{0:T(1024)(128)(4,1)S(1)} %iota_compare_fusion, bf16[1024,4,80]{0,2,1:T(8,128)(2,1)} %bitcast.76, bf16[1024,4,80]{0,2,1:T(8,128)(2,1)} %bitcast.75), kind=kOutput, calls=%fused_computation.150 | convolution fusion | flops 687866880 | bytes 18105344 | tf_op jit(solution)/shard_map/sub | solution.py:49
  28.1 7.6 %fusion.20 = bf16[4,80,1024]{2,1,0:T(8,128)(2,1)S(1)} fusion(bf16[1024,4,80]{0,2,1:T(8,128)(2,1)} %bitcast.74, f32[4,1024,1024]{1,2,0:T(8,128)} %get-tuple-element.17, f32[4,1024]{1,0:T(4,128)S(1)} %get-tuple-element.16), kind=kOutput, calls=%fused_computation.33 | convolution fusion | flops 679804928 | bytes 18104320 | tf_op jit(solution)/shard_map/ihqk,ikhd->iqhd/dot_general | solution.py:51
  35.8 3.1 convolution_convert_fusion.2
  39.1 62.5 %all-reduce.2.cloned.1.call-done = bf16[1024,1280]{1,0:T(8,128)(2,1)} async-done(((bf16[1024,1280]{1,0:T(8,128)(2,1)}), bf16[1024,1280]{1,0:T(8,128)(2,1)}) %all-reduce.2.cloned.1.call-update) | async-done | bytes 2621456 | tf_op jit(solution)/shard_map/psum | solution.py:58
  101.6 3.8 multiply_reduce_fusion
  105.7 2.6 multiply_convert_fusion
  108.4 5.6 all_to_all.25
  113.9 2.1 copy.26
  116.0 63.7 %all_to_all.33 = bf16[256,4,1280]{2,0,1:T(8,128)(2,1)S(1)} all-to-all(bf16[256,4,1280]{2,0,1:T(8,128)(2,1)S(1)} %copy.26), channel_id=1, replica_groups=mesh['groups'=2,'dp'=4,'tensor'=4] {'dp'}, dimensions={1} | all-to-all | bytes 5242880 | tf_op jit(solution)/shard_map/all_to_all | solution.py:63
  179.7 4.9 convolution_convert_fusion.1
  185.4 50.1 %reduce-scatter.3.cloned.1.call-done = bf16[256,1280]{1,0:T(8,128)(2,1)} async-done(((bf16[1024,1280]{1,0:T(8,128)(2,1)}), bf16[256,1280]{1,0:T(8,128)(2,1)}) %reduce-scatter.3.cloned.1.call-update) | async-done | bytes 655376 | tf_op jit(solution)/shard_map/reduce_scatter | solution.py:64
  235.5 358.2 %all-gather.2.cloned.1.call-done = bf16[1280,8192]{1,0:T(8,128)(2,1)} async-done(((bf16[1280,2048]{1,0:T(8,128)(2,1)}), bf16[1280,8192]{1,0:T(8,128)(2,1)}) %all-gather.2.cloned.1.call-update) | async-done | bytes 20971536 | tf_op jit(solution)/shard_map/all_gather | solution.py:73
  593.7 17.4 %convolution_convert_fusion = bf16[256,8192]{1,0:T(8,128)(2,1)} fusion(bf16[1280,8192]{1,0:T(8,128)(2,1)} %all-gather.2.cloned.1.call-done, bf16[256,1280]{1,0:T(8,128)(2,1)} %reduce-scatter.3.cloned.1.call-done, f32[1280]{0:T(1024)S(1)} %copy-done.13), kind=kOutput, calls=%fused_computation.8 | convolution fusion | flops 5392760832 | bytes 25826304 | tf_op jit(solution)/shard_map/dot_general | solution.py:71
  611.8 1.2 reduce-window.6
  614.1 38.8 %scatter_fusion = s32[4,64]{1,0:T(4,128)} fusion(s32[4,64]{1,0:T(4,128)} %broadcast_in_dim.23, s32[256]{0:T(256)S(1)} %bitcast.71, s32[256]{0:T(256)S(1)} %get-tuple-element.10), kind=kCustom, calls=%fused_computation | custom fusion | bytes 5120 | tf_op jit(solution)/shard_map/scatter | solution.py:103
  652.9 3.2 all-to-all-start
  656.1 1.5 add_convert_fusion.1
  658.8 47.9 %scatter_fusion.1 = bf16[4,64,2048]{2,1,0:T(8,128)(2,1)} fusion(bf16[4,64,2048]{2,1,0:T(8,128)(2,1)} %broadcast_in_dim.28, s32[256]{0:T(256)S(1)} %bitcast.72, bf16[256,2048]{1,0:T(8,128)(2,1)S(1)} %add_convert_fusion.1), kind=kCustom, calls=%fused_computation.1 | custom fusion | bytes 3147776 | tf_op jit(solution)/shard_map/scatter | solution.py:98
  706.6 4.8 all-to-all-start.2
  712.7 24.3 %all-to-all-done.2 = bf16[4,64,2048]{2,1,0:T(8,128)(2,1)} async-done(((bf16[4,64,2048]{2,1,0:T(8,128)(2,1)}), bf16[4,64,2048]{2,1,0:T(8,128)(2,1)}, u32[]{:S(2)}, u32[]{:S(2)}) %all-to-all-start.2) | async-done | bytes 1048608 | tf_op jit(solution)/shard_map/all_to_all | solution.py:106
  737.0 5.7 scatter_fusion.2
  (64 shorter events, 7.8 us)
Async XLA Ops:
  6.5 173.2 %copy-start = (bf16[1280,1280]{1,0:T(8,128)(2,1)S(1)}, bf16[1280,1280]{1,0:T(8,128)(2,1)}, u32[]{:S(2)}) copy-start(bf16[1280,1280]{1,0:T(8,128)(2,1)} %param.23) | copy-start | bytes 9830404
  6.5 2.9 copy-start.9
  6.5 95.1 %all-reduce.2.cloned.1.call-start = ((), (), s32[]{:S(2)}) async-start(), calls=%async_computation.5 | async-start | bytes 5242880 | tf_op jit(solution)/shard_map/psum | solution.py:58
  6.5 4.8 copy-start.2
  11.4 1.7 copy-start.10
  11.4 1.7 copy-start.12
  11.4 1.7 copy-start.14
  28.1 7.6 %copy-start.11 = (bf16[320,1280]{1,0:T(8,128)(2,1)S(1)}, bf16[320,1280]{1,0:T(8,128)(2,1)}, u32[]{:S(2)}) copy-start(bf16[320,1280]{1,0:T(8,128)(2,1)} %param.20) | copy-start | bytes 2457604
  38.9 62.8 %copy-start.5 = (f32[1280]{0:T(1024)S(1)}, f32[1280]{0:T(1024)}, u32[]{:S(2)}) copy-start(f32[1280]{0:T(1024)} %param.21) | copy-start | bytes 15364
  38.9 66.5 %copy-start.7 = (f32[1280]{0:T(1024)S(1)}, f32[1280]{0:T(1024)}, u32[]{:S(2)}) copy-start(f32[1280]{0:T(1024)} %param.22) | copy-start | bytes 15364
  38.9 196.6 %reduce-scatter.3.cloned.1.call-start = ((), (), s32[]{:S(2)}) async-start(), calls=%async_computation.6 | async-start | bytes 3276800 | tf_op jit(solution)/shard_map/reduce_scatter | solution.py:64
  101.6 3.8 copy-start.3
  101.6 4.1 copy-start.4
  184.6 409.1 %copy-start.13 = (f32[1280]{0:T(1024)S(1)}, f32[1280]{0:T(1024)}, u32[]{:S(2)}) copy-start(f32[1280]{0:T(1024)} %param.24) | copy-start | bytes 15364
  184.6 409.0 %all-gather.2.cloned.1.call-start = ((), (), s32[]{:S(2)}) async-start(), calls=%async_computation.7 | async-start | bytes 26214400 | tf_op jit(solution)/shard_map/all_gather | solution.py:73
  185.4 470.7 %reduce-scatter.5.cloned.1.call-start = ((), (), s32[]{:S(2)}) async-start(), calls=%async_computation.8 | async-start | bytes 5242880 | tf_op jit(solution)/shard_map/reduce_scatter | solution.py:76
  611.1 0.7 copy-start.6
  611.1 45.0 %copy-start.8 = (f32[2048]{0:T(1024)S(1)}, f32[2048]{0:T(1024)}, u32[]{:S(2)}) copy-start(f32[2048]{0:T(1024)} %param.26) | copy-start | bytes 24580
  652.9 53.8 %all-to-all-start = ((s32[4,1,64]{2,1,0:T(1,128)}), s32[4,1,64]{2,1,0:T(1,128)S(1)}, u32[]{:S(2)}, u32[]{:S(2)}) async-start(s32[4,1,64]{2,1,0:T(1,128)} %bitcast.12), calls=%async_computation | async-start | bytes 4096 | tf_op jit(solution)/shard_map/all_to_all | solution.py:107
  706.6 30.4 %all-to-all-start.2 = ((bf16[4,64,2048]{2,1,0:T(8,128)(2,1)}), bf16[4,64,2048]{2,1,0:T(8,128)(2,1)}, u32[]{:S(2)}, u32[]{:S(2)}) async-start(bf16[4,64,2048]{2,1,0:T(8,128)(2,1)} %scatter_fusion.1), calls=%async_computation.4 | async-start | bytes 2097152 | tf_op jit(solution)/shard_map/all_to_all | solution.py:106
  737.0 5.7 copy-start.1
Sparse Core Ops, SparseCore 0:
  39.0 62.5 all-reduce.1
  184.7 50.7 reduce-scatter.2
  237.1 356.5 all-gather.1
  611.2 43.0 reduce-scatter.4
where the time goes:
time: 753 us; the launch traced here: 749 us
  waiting for transfers between devices  496 us (66%)
  local copies, waits for them, and re-layouts  110 us (15%)
  blocking collectives  63.7 us (8%)
  matrix products  46.7 us (6%)
  between operations  14.6 us (2%)
  other arithmetic  10.6 us (1%)
  starting transfers between devices  8.27 us (1%)
    all_gather x1, waiting for transfers between devices, local(): lax.all_gather(w_second, 'dp', axis=1, tiled=True)  358 us
    all_to_all x1, blocking collectives, local(): lax.all_to_all(merged_in, 'dp', split_axis=1, concat_axis=0, tiled=True)  63.7 us
    psum x1, waiting for transfers between devices, local(): summed = lax.psum(partial_value, 'tensor').astype(jnp.float32)  62.5 us
    reduce_scatter x1, waiting for transfers between devices, local(): lax.psum_scatter(jnp.dot(received, w_first, preferred_element_type=jnp.fl...  50.1 us
    scatter x1, local copies, waits for them, and re-layouts, local(): buffer = jnp.zeros((dp_count, capacity, feature_count), jnp.bfloat16).at[...  47.9 us
    scatter x1, local copies, waits for them, and re-layouts, local(): positions = jnp.full((dp_count, capacity), seq_rows, jnp.int32).at[shard_...  38.8 us
    all_to_all x1, waiting for transfers between devices, local(): lax.all_to_all(buffer, 'dp', split_axis=0, concat_axis=0, tiled=True)  24.3 us
    dot_general x1, matrix products, local(): jnp.dot(hidden, lax.all_gather(w_second, 'dp', axis=1, tiled=True), prefe...  17.4 us
  transfers between devices with their start and end apart: 6, of which 4 were waited for; matrix products, arithmetic and copies ran while one was open for 12% of the time, Pallas kernels for 0%

commit v1 on v0

v1 whole, which is shorter than its diff:
```python
import math

import jax
import jax.numpy as jnp
from jax import lax
from jax.sharding import PartitionSpec as P

HEAD_DIM = 80
MERGE = 4


def rms_scale(values, gain):
    return values * lax.rsqrt(jnp.mean(values * values, axis=-1, keepdims=True) + 1e-06) * gain


def dot32(a, b):
    return jnp.dot(a, b, preferred_element_type=jnp.float32)


def swap(x, axis, k):
    n = lax.axis_size(axis)
    return lax.ppermute(x, axis, [(a, a ^ k) for a in range(n)])


def gather_xor(x, axis):
    n = lax.axis_size(axis)
    blocks = {0: x}
    step = n // 2
    while step:
        for k in list(blocks):
            blocks[k | step] = swap(blocks[k], axis, step)
        step //= 2
    return [blocks[k] for k in range(n)]


def scatter_sum_xor(blocks, axis):
    n = lax.axis_size(axis)
    blocks = dict(enumerate(blocks))
    step = 1
    while step < n:
        for k in sorted(blocks):
            if k & step:
                got = swap(blocks[k], axis, step)
                mine = k ^ step
                blocks[mine] = (
                    blocks[mine].astype(jnp.float32) + got.astype(jnp.float32)
                ).astype(got.dtype)
        blocks = {k: v for k, v in blocks.items() if not k & step}
        step *= 2
    return blocks[0]


def slots(target, seq_rows, shards):
    shard = jnp.where(target >= 0, target // seq_rows, shards)
    same = shard[..., :, None] == shard[..., None, :]
    count = target.shape[-1]
    earlier = jnp.arange(count)[None, :] < jnp.arange(count)[:, None]
    rank = jnp.sum((same & earlier).astype(jnp.int32), axis=-1)
    return shard, rank


def local(
    patches,
    grids,
    dest,
    norm_gain,
    qkv_weight,
    qkv_bias,
    proj_weight,
    proj_bias,
    merge_gain,
    w_first,
    b_first,
    w_second,
    b_second,
    text_embed,
):
    dps, tensors = lax.axis_size("dp"), lax.axis_size("tensor")
    tensor_at, dp_at = lax.axis_index("tensor"), lax.axis_index("dp")
    rows, width = patches.shape
    merged = dest.shape[1]
    seq_rows = text_embed.shape[0]
    heads = qkv_weight.shape[2] // HEAD_DIM
    cap = merged // dps
    part = cap // tensors

    live = grids[0, 0] * grids[0, 1]
    target = jnp.where(jnp.arange(merged, dtype=jnp.int32) < live // MERGE, dest[0], -1)
    targets = lax.all_gather(target, "dp", axis=0)
    proj_blocks = gather_xor(proj_weight, "tensor")

    shard, rank = slots(target, seq_rows, dps)
    order = jnp.arange(rows, dtype=jnp.int32)
    slot_of = order % part
    shard_of = order // part % dps
    patch_of = order // (part * dps) % MERGE
    rank_of = order // (part * dps * MERGE) * part + slot_of
    row_shard = jnp.repeat(shard, MERGE)
    row_rank = jnp.repeat(rank, MERGE)
    row_patch = jnp.tile(jnp.arange(MERGE, dtype=jnp.int32), merged)
    place = (
        (shard_of[:, None] == row_shard[None, :])
        & (rank_of[:, None] == row_rank[None, :])
        & (patch_of[:, None] == row_patch[None, :])
    ).astype(jnp.bfloat16)

    normed = rms_scale(patches.astype(jnp.float32), norm_gain).astype(jnp.bfloat16)
    projected = (
        jnp.einsum("rv,jvc->jrc", normed, qkv_weight, preferred_element_type=jnp.float32)
        + qkv_bias[:, None, :]
    )
    projected = projected.astype(jnp.bfloat16).reshape(3, rows, heads, HEAD_DIM)
    scores = jnp.einsum(
        "qhd,khd->hqk", projected[0], projected[1], preferred_element_type=jnp.float32
    ) / math.sqrt(HEAD_DIM)
    live_keys = jnp.arange(rows, dtype=jnp.int32) < live
    scores = jnp.where(live_keys[None, None, :], scores, jnp.float32(-1e30))
    peak_score = jnp.max(scores, axis=-1, keepdims=True)
    exponent = jnp.exp(scores - peak_score)
    weights = (exponent / jnp.sum(exponent, axis=-1, keepdims=True)).astype(jnp.bfloat16)
    attended = jnp.einsum("hqk,khd->qhd", weights, projected[2], preferred_element_type=jnp.float32)
    attended = attended.astype(jnp.bfloat16).reshape(rows, heads * HEAD_DIM)

    attended = dot32(place, attended).astype(jnp.bfloat16)
    attended = attended.reshape(tensors, rows // tensors, heads * HEAD_DIM)
    place = place.reshape(tensors, rows // tensors, rows)
    summed = None
    for k in range(tensors):
        block = lax.dynamic_index_in_dim(attended, tensor_at ^ k, 0, keepdims=False)
        if k:
            block = swap(block, "tensor", k)
        term = dot32(block, proj_blocks[k])
        summed = term if summed is None else summed + term
    own = dot32(lax.dynamic_index_in_dim(place, tensor_at, 0, keepdims=False), patches)
    resid = own + summed + proj_bias
    merged_in = rms_scale(resid, merge_gain).astype(jnp.bfloat16)

    piece = w_first.shape[0]
    splits = width // piece
    merged_in = merged_in.reshape(MERGE, dps * part, splits, piece).transpose(0, 2, 1, 3)
    merged_in = merged_in.reshape(dps, dps * part, piece)
    received = lax.all_to_all(merged_in, "dp", split_axis=0, concat_axis=0, tiled=True)
    received = received.reshape(dps * dps * part, piece)
    received = jnp.concatenate(gather_xor(received, "tensor"), axis=0)

    first_part = dot32(received, w_first).astype(jnp.bfloat16)
    first_out = lax.psum(first_part, "dp").astype(jnp.float32)
    hidden = jax.nn.gelu(first_out + b_first, approximate=False).astype(jnp.bfloat16)

    second_part = dot32(hidden, w_second).astype(jnp.bfloat16)
    columns = w_second.shape[1]
    second_part = second_part.reshape(tensors, dps * dps * part, columns)
    visual = scatter_sum_xor([second_part[k] for k in range(tensors)], "tensor")
    visual = visual.reshape(dps, dps, part, columns).transpose(1, 0, 2, 3)
    visual = lax.all_to_all(visual, "dp", split_axis=0, concat_axis=0, tiled=True)
    shares = dps // tensors
    visual = visual.reshape(tensors, shares, dps * part, columns).transpose(0, 2, 1, 3)
    visual = visual.reshape(tensors, dps * part, shares * columns)
    visual = lax.all_to_all(visual, "tensor", split_axis=0, concat_axis=0, tiled=True)
    visual = visual.reshape(tensors * dps * part, shares * columns)

    all_shard, all_rank = slots(targets, seq_rows, dps)
    mine = all_shard == dp_at
    slot_rows = jnp.sum(
        jnp.where(
            mine[:, None, :] & (all_rank[:, None, :] == jnp.arange(cap)[None, :, None]),
            targets[:, None, :] % seq_rows + 1,
            0,
        ),
        axis=-1,
    )
    slot_rows = slot_rows.reshape(dps, tensors, part).transpose(1, 0, 2).reshape(-1) - 1
    hit = jnp.arange(seq_rows, dtype=jnp.int32)[:, None] == slot_rows[None, :]
    covered = jnp.any(hit, axis=1)
    placed = dot32(hit.astype(jnp.bfloat16), visual) + b_second
    return jnp.where(covered[:, None], placed.astype(jnp.bfloat16), text_embed)


def solution(mesh):
    in_specs = (
        P(("groups", "dp"), None),
        P(("groups", "dp"), None),
        P(("groups", "dp"), None),
        P(),
        P(None, None, "tensor"),
        P(None, "tensor"),
        P("tensor", None),
        P(),
        P(),
        P("dp", "tensor"),
        P("tensor"),
        P("tensor", "dp"),
        P("tensor"),
        P(("groups", "dp"), "tensor"),
    )
    out_specs = P(("groups", "dp"), "tensor")
    return jax.shard_map(local, mesh=mesh, in_specs=in_specs, out_specs=out_specs, check_vma=False)
```

time: 753 us -> 320 us (0.42)
  waiting for transfers between devices: 496 us -> 163 us
  local copies, waits for them, and re-layouts: 110 us -> 10.5 us
  blocking collectives: 63.7 us -> 45.3 us
  matrix products: 46.7 us -> 63.2 us
  starting transfers between devices: 8.27 us -> 17.1 us
    all_gather x1 -> x0, waiting for transfers between devices: 358 us -> none  [local(): lax.all_gather(w_second, 'dp', axis=1, tiled=True)]
    scatter x3 -> x0, local copies, waits for them, and re-layouts: 92.3 us -> none  [the longest x1 47.9 us: local(): buffer = jnp.zeros((dp_count, capacity, feature_count), jnp.bfloat16).at[...]
    reduce_scatter x2 -> x0, waiting for transfers between devices: 50.1 us -> none  [the longest x1 50.1 us: local(): lax.psum_scatter(jnp.dot(received, w_first, preferred_element_type=jnp.fl...]
    ppermute x0 -> x12, waiting for transfers between devices: none -> 43.3 us  [swap(): return lax.ppermute(x, axis, [(a, a ^ k) for a in range(n)])]
    all_to_all x1, blocking collectives: 63.7 us -> 22.6 us  [local(): lax.all_to_all(merged_in, 'dp', split_axis=0, concat_axis=0, tiled=True)]
    psum x1, waiting for transfers between devices: 62.5 us -> 103 us  [local(): first_out = lax.psum(first_part, 'dp').astype(jnp.float32)]
    all_gather x0 -> x1, blocking collectives: none -> 22.7 us  [local(): targets = lax.all_gather(target, 'dp', axis=0)]
    dot_general x4 -> x10, matrix products: 33 us -> 46.8 us  [the longest x9 39.2 us: dot32(): return jnp.dot(a, b, preferred_element_type=jnp.float32)]
  transfers between devices with their start and end apart: 6 -> 15, of which waited for: 4 -> 8; matrix products, arithmetic and copies ran while one was open for 12% -> 15% of each run, Pallas kernels for 0% -> 0%
where the time goes in v1:
time: 320 us; the launch traced here: 319 us
  waiting for transfers between devices  163 us (51%)
  matrix products  63.2 us (20%)
  blocking collectives  45.3 us (14%)
  starting transfers between devices  17.1 us (5%)
  between operations  15 us (5%)
  local copies, waits for them, and re-layouts  10.5 us (3%)
  other arithmetic  5.85 us (2%)
    psum x1, waiting for transfers between devices, local(): first_out = lax.psum(first_part, 'dp').astype(jnp.float32)  103 us
    ppermute x12, waiting for transfers between devices, swap(): return lax.ppermute(x, axis, [(a, a ^ k) for a in range(n)])  43.3 us
    dot_general x9, matrix products, dot32(): return jnp.dot(a, b, preferred_element_type=jnp.float32)  39.2 us
    all_gather x1, blocking collectives, local(): targets = lax.all_gather(target, 'dp', axis=0)  22.7 us
    all_to_all x1, blocking collectives, local(): lax.all_to_all(merged_in, 'dp', split_axis=0, concat_axis=0, tiled=True)  22.6 us
    all_to_all x1, waiting for transfers between devices, local(): lax.all_to_all(visual, 'tensor', split_axis=0, concat_axis=0, tiled=True)  13.6 us
    sub x1, matrix products, local(): exponent = jnp.exp(scores - peak_score)  11.1 us
    ppermute x12, starting transfers between devices, swap(): return lax.ppermute(x, axis, [(a, a ^ k) for a in range(n)])  8.45 us
  transfers between devices with their start and end apart: 15, of which 8 were waited for; matrix products, arithmetic and copies ran while one was open for 15% of the time, Pallas kernels for 0%

profile of v1, /device:TPU:0, one launch (start us, length us, event | category | flops | bytes accessed | tf_op | source)
XLA Modules:
  0.0 319.5 jit_solution(4429873735781219476)
XLA Ops:
  7.0 2.5 collective-permute-start.3
  14.2 2.3 fusion.6
  16.5 5.3 %fusion.81 = bf16[3,1024,320]{1,2,0:T(8,128)(2,1)S(1)} fusion(f32[3,320]{1,0:T(4,128)} %param.19, bf16[3,1280,320]{1,2,0:T(8,128)(2,1)} %param.18, bf16[1024,1280]{1,0:T(8,128)(2,1)} %param.14, f32[1280]{0:T(1024)} %param.17, f32[1024]{0:T(1024)S(1)} %add_rsqrt_fusion), kind=kOutput, calls=%fused_computation.103 | convolution fusion | flops 2523791360 | bytes 7058176 | tf_op jit(solution)/shard_map/rv,jvc->jrc/dot_general | solution.py:109
  23.3 11.1 %fusion.175 = (f32[4,1024]{1,0:T(4,128)S(1)}, f32[4,1024,1024]{1,2,0:T(8,128)}) fusion(pred[1024]{0:T(1024)(128)(4,1)S(1)} %iota_compare_fusion.4, bf16[1024,4,80]{0,2,1:T(8,128)(2,1)} %bitcast.96, bf16[1024,4,80]{0,2,1:T(8,128)(2,1)} %bitcast.95), kind=kOutput, calls=%fused_computation.258 | convolution fusion | flops 687866880 | bytes 18105344 | tf_op jit(solution)/shard_map/sub | solution.py:119
  34.4 7.6 %fusion.89 = bf16[4,80,1024]{2,1,0:T(8,128)(2,1)S(1)} fusion(bf16[1024,4,80]{0,2,1:T(8,128)(2,1)} %bitcast.94, f32[4,1024,1024]{1,2,0:T(8,128)} %get-tuple-element.21, f32[4,1024]{1,0:T(4,128)S(1)} %get-tuple-element.20), kind=kOutput, calls=%fused_computation.106 | convolution fusion | flops 679804928 | bytes 18104320 | tf_op jit(solution)/shard_map/hqk,khd->qhd/dot_general | solution.py:121
  42.0 2.6 fusion.86
  44.6 2.5 reshape.234
  47.0 3.3 %constant_dynamic-slice_fusion.1 = (bf16[1,256,320]{1,0,2:T(2,128)(2,1)S(1)}, bf16[1,256,320]{1,0,2:T(2,128)(2,1)S(1)}, bf16[1,256,320]{1,0,2:T(2,128)(2,1)S(1)}, bf16[1,256,320]{1,0,2:T(2,128)(2,1)S(1)}) fusion(bf16[4,256,320]{1,0,2:T(4,128)(2,1)} %reshape.234, s32[]{:T(128)S(6)} %select_n.176, s32[]{:T(128)S(6)} %select_n.175, s32[]{:T(128)S(6)} %select_n.174, ...), kind=kLoop, calls=%fused_computation.213 | loop fusion | bytes 1310736 | tf_op jit(solution)/shard_map/jit(dynamic_index_in_dim)/dynamic_slice | solution.py:129
  52.6 2.7 fusion.90
  58.2 1.7 convolution_add_fusion.1
  60.8 22.6 %all_to_all.15 = bf16[4,64,1280]{2,1,0:T(8,128)(2,1)S(1)} all-to-all(bf16[4,64,1280]{2,1,0:T(8,128)(2,1)S(1)} %bitcast.90), channel_id=1, replica_groups=mesh['groups'=2,'dp'=4,'tensor'=4] {'dp'}, dimensions={0} | all-to-all | bytes 1310720 | tf_op jit(solution)/shard_map/all_to_all | solution.py:142
  84.2 15.2 %collective-permute-done.7 = bf16[256,1280]{1,0:T(8,128)(2,1)S(1)} collective-permute-done((bf16[256,1280]{1,0:T(8,128)(2,1)S(1)}, bf16[256,1280]{1,0:T(8,128)(2,1)S(1)}, u32[]{:S(2)}, u32[]{:S(2)}) %collective-permute-start.7) | collective-permute-done | bytes 655392 | tf_op jit(solution)/shard_map/ppermute | solution.py:22
  99.5 2.1 collective-permute-done.8
  101.6 6.6 %convolution_convert_fusion.1 = bf16[1024,1280]{1,0:T(8,128)(2,1)} fusion(bf16[1280,1280]{1,0:T(8,128)(2,1)S(1)} %copy-done, bf16[256,1280]{1,0:T(8,128)(2,1)S(1)} %collective-permute-done.8, bf16[256,1280]{1,0:T(8,128)(2,1)S(1)} %collective-permute-done.7, bf16[256,1280]{1,0:T(8,128)(2,1)S(1)} %collective-permute-done.6, bf16[256,1280]{1,0:T(8,128)(2,1)S(1)} %bitcast.93), kind=kOutput, calls=%fused_computation.44 | convolution fusion | flops 3367239680 | bytes 8519680 | tf_op jit(solution)/shard_map/dot_general | solution.py:17
  108.2 102.7 %all-reduce.2.cloned.1.call-done = bf16[1024,1280]{1,0:T(8,128)(2,1)} async-done(((bf16[1024,1280]{1,0:T(8,128)(2,1)}), bf16[1024,1280]{1,0:T(8,128)(2,1)}) %all-reduce.2.cloned.1.call-update) | async-done | bytes 2621456 | tf_op jit(solution)/shard_map/psum | solution.py:147
  211.0 19.2 %convolution_convert_fusion = bf16[1024,2048]{1,0:T(8,128)(2,1)S(1)} fusion(bf16[1280,2048]{1,0:T(8,128)(2,1)} %param.25, bf16[1024,1280]{1,0:T(8,128)(2,1)} %all-reduce.2.cloned.1.call-done, f32[1280]{0:T(1024)S(1)} %copy-done.5), kind=kOutput, calls=%fused_computation.43 | convolution fusion | flops 5458624512 | bytes 12063744 | tf_op jit(solution)/shard_map/dot_general | solution.py:17
  231.0 2.1 collective-permute-done.10
  235.1 23.7 %collective-permute-done.11 = bf16[256,2048]{1,0:T(8,128)(2,1)S(1)} collective-permute-done((bf16[256,2048]{1,0:T(8,128)(2,1)S(1)}, bf16[256,2048]{1,0:T(8,128)(2,1)S(1)}, u32[]{:S(2)}, u32[]{:S(2)}) %collective-permute-start.11) | collective-permute-done | bytes 1048608 | tf_op jit(solution)/shard_map/ppermute | solution.py:22
  260.4 4.4 %all-to-all-start.1 = ((bf16[4,4,16,2048]{3,2,1,0:T(8,128)(2,1)}), bf16[4,4,16,2048]{3,2,1,0:T(8,128)(2,1)}, u32[]{:S(2)}, u32[]{:S(2)}) async-start(bf16[4,4,16,2048]{3,2,1,0:T(8,128)(2,1)} %bitcast.88), calls=%async_computation.1 | async-start | bytes 2097152 | tf_op jit(solution)/shard_map/all_to_all | solution.py:155
  264.8 22.7 %all-gather = s32[4,1,256]{2,1,0:T(1,128)S(1)} all-gather(s32[1,1,256]{2,1,0:T(1,128)S(1)} %get-tuple-element.16), channel_id=1, replica_groups=mesh['groups'=2,'dp'=4,'tensor'=4] {'dp'}, dimensions={0}, use_global_device_ids=true | all-gather | bytes 5120 | tf_op jit(solution)/shard_map/all_gather | solution.py:89
  287.5 2.8 all-to-all-done.1
  290.3 4.3 %all-to-all-start.2 = ((bf16[4,64,2048]{2,1,0:T(8,128)(2,1)}), bf16[4,64,2048]{2,1,0:T(8,128)(2,1)}, u32[]{:S(2)}, u32[]{:S(2)}) async-start(bf16[4,64,2048]{2,1,0:T(8,128)(2,1)} %bitcast.24), calls=%async_computation.2 | async-start | bytes 2097152 | tf_op jit(solution)/shard_map/all_to_all | solution.py:159
  295.5 13.6 %all-to-all-done.2 = bf16[4,64,2048]{2,1,0:T(8,128)(2,1)} async-done(((bf16[4,64,2048]{2,1,0:T(8,128)(2,1)}), bf16[4,64,2048]{2,1,0:T(8,128)(2,1)}, u32[]{:S(2)}, u32[]{:S(2)}) %all-to-all-start.2) | async-done | bytes 1048608 | tf_op jit(solution)/shard_map/all_to_all | solution.py:159
  309.1 3.5 %fusion.74 = bf16[384,2048]{1,0:T(8,128)(2,1)} fusion(bf16[384,2048]{1,0:T(8,128)(2,1)} %param.27, bf16[256,2048]{1,0:T(8,128)(2,1)} %bitcast.25, f32[2048]{0:T(1024)S(1)} %copy-done.6, pred[384]{0:T(512)(128)(4,1)S(1)} %fusion.103, s32[256]{0:T(256)S(1)} %sub.61), kind=kOutput, calls=%fused_computation.93 | convolution fusion | flops 405110784 | bytes 4203904 | tf_op jit(solution)/shard_map/dot_general | solution.py:17
  (78 shorter events, 17.3 us)
Async XLA Ops:
  6.5 95.0 %copy-start = (bf16[1280,1280]{1,0:T(8,128)(2,1)S(1)}, bf16[1280,1280]{1,0:T(8,128)(2,1)}, u32[]{:S(2)}) copy-start(bf16[1280,1280]{1,0:T(8,128)(2,1)} %param.23) | copy-start | bytes 9830404
  6.5 204.4 %all-reduce.2.cloned.1.call-start = ((), (), s32[]{:S(2)}) async-start(), calls=%async_computation.3 | async-start | bytes 5242880 | tf_op jit(solution)/shard_map/psum | solution.py:147
  6.5 49.9 %collective-permute-start.1 = (bf16[320,1280]{1,0:T(8,128)(2,1)}, bf16[320,1280]{1,0:T(8,128)(2,1)}, u32[]{:S(2)}, u32[]{:S(2)}) collective-permute-start(bf16[320,1280]{1,0:T(8,128)(2,1)} %param.20), channel_id=1, source_target_pairs={{0,1},{1,0},{2,3},{3,2},{4,5},{5,4},{6,7},{7,6},{8,9},{9,8},{10,11... | collective-permute-start | bytes 2457608 | tf_op jit(solution)/shard_map/ppermute | solution.py:22
  7.0 48.3 %collective-permute-start.3 = (bf16[320,1280]{1,0:T(8,128)(2,1)}, bf16[320,1280]{1,0:T(8,128)(2,1)}, u32[]{:S(2)}, u32[]{:S(2)}) collective-permute-start(bf16[320,1280]{1,0:T(8,128)(2,1)} %param.20), channel_id=1, source_target_pairs={{0,2},{1,3},{2,0},{3,1},{4,6},{5,7},{6,4},{7,5},{8,10},{9,11},{10,... | collective-permute-start | bytes 2457608 | tf_op jit(solution)/shard_map/ppermute | solution.py:22
  47.0 8.9 %copy-start.2 = (bf16[320,1280]{1,0:T(8,128)(2,1)S(1)}, bf16[320,1280]{1,0:T(8,128)(2,1)}, u32[]{:S(2)}) copy-start(bf16[320,1280]{1,0:T(8,128)(2,1)} %param.20) | copy-start | bytes 2457604
  50.4 6.1 %collective-permute-start = (bf16[256,320]{0,1:T(8,128)(2,1)S(1)}, bf16[256,320]{0,1:T(8,128)(2,1)S(1)}, u32[]{:S(2)}, u32[]{:S(2)}) collective-permute-start(bf16[256,320]{0,1:T(8,128)(2,1)S(1)} %bitcast.99), channel_id=1, source_target_pairs={{0,1},{1,0},{2,3},{3,2},{4,5},{5,4},{6,7},{7,6},{8,9},{9,8},{10,11... | collective-permute-start | bytes 491528 | tf_op jit(solution)/shard_map/ppermute | solution.py:22
  50.7 7.5 %collective-permute-start.2 = (bf16[256,320]{0,1:T(8,128)(2,1)S(1)}, bf16[256,320]{0,1:T(8,128)(2,1)S(1)}, u32[]{:S(2)}, u32[]{:S(2)}) collective-permute-start(bf16[256,320]{0,1:T(8,128)(2,1)S(1)} %bitcast.98), channel_id=1, source_target_pairs={{0,2},{1,3},{2,0},{3,1},{4,6},{5,7},{6,4},{7,5},{8,10},{9,11},{10,... | collective-permute-start | bytes 491528 | tf_op jit(solution)/shard_map/ppermute | solution.py:22
  51.3 8.7 %collective-permute-start.4 = (bf16[256,320]{0,1:T(8,128)(2,1)S(1)}, bf16[256,320]{0,1:T(8,128)(2,1)S(1)}, u32[]{:S(2)}, u32[]{:S(2)}) collective-permute-start(bf16[256,320]{0,1:T(8,128)(2,1)S(1)} %bitcast.97), channel_id=1, source_target_pairs={{0,3},{1,2},{2,1},{3,0},{4,7},{5,6},{6,5},{7,4},{8,11},{9,10},{10,... | collective-permute-start | bytes 491528 | tf_op jit(solution)/shard_map/ppermute | solution.py:22
  55.3 4.7 %copy-start.3 = (f32[1280]{0:T(1024)S(1)}, f32[1280]{0:T(1024)}, u32[]{:S(2)}) copy-start(f32[1280]{0:T(1024)} %param.21) | copy-start | bytes 15364
  55.3 4.6 %collective-permute-start.5 = (bf16[320,1280]{1,0:T(8,128)(2,1)}, bf16[320,1280]{1,0:T(8,128)(2,1)S(1)}, u32[]{:S(2)}, u32[]{:S(2)}) collective-permute-start(bf16[320,1280]{1,0:T(8,128)(2,1)} %collective-permute-done.3), channel_id=1, source_target_pairs={{0,1},{1,0},{2,3},{3,2},{4,5},{5,4},{6,7},{7,6},{8,9},{9,8},{10,11... | collective-permute-start | bytes 2457608 | tf_op jit(solution)/shard_map/ppermute | solution.py:22
  56.5 4.2 %copy-start.4 = (f32[1280]{0:T(1024)S(1)}, f32[1280]{0:T(1024)}, u32[]{:S(2)}) copy-start(f32[1280]{0:T(1024)} %param.22) | copy-start | bytes 15364
  83.5 127.5 %copy-start.5 = (f32[1280]{0:T(1024)S(1)}, f32[1280]{0:T(1024)}, u32[]{:S(2)}) copy-start(f32[1280]{0:T(1024)} %param.24) | copy-start | bytes 15364
  83.5 16.0 %collective-permute-start.7 = (bf16[256,1280]{1,0:T(8,128)(2,1)S(1)}, bf16[256,1280]{1,0:T(8,128)(2,1)S(1)}, u32[]{:S(2)}, u32[]{:S(2)}) collective-permute-start(bf16[256,1280]{1,0:T(8,128)(2,1)S(1)} %bitcast.91), channel_id=1, source_target_pairs={{0,2},{1,3},{2,0},{3,1},{4,6},{5,7},{6,4},{7,5},{8,10},{9,11},{10,... | collective-permute-start | bytes 1966088 | tf_op jit(solution)/shard_map/ppermute | solution.py:22
  84.2 15.3 %collective-permute-start.6 = (bf16[256,1280]{1,0:T(8,128)(2,1)S(1)}, bf16[256,1280]{1,0:T(8,128)(2,1)S(1)}, u32[]{:S(2)}, u32[]{:S(2)}) collective-permute-start(bf16[256,1280]{1,0:T(8,128)(2,1)S(1)} %bitcast.92), channel_id=1, source_target_pairs={{0,1},{1,0},{2,3},{3,2},{4,5},{5,4},{6,7},{7,6},{8,9},{9,8},{10,11... | collective-permute-start | bytes 1966088 | tf_op jit(solution)/shard_map/ppermute | solution.py:22
  99.5 2.1 collective-permute-start.8
  230.4 2.7 collective-permute-start.10
  230.5 4.6 %collective-permute-start.9 = (bf16[256,2048]{1,0:T(8,128)(2,1)S(1)}, bf16[256,2048]{1,0:T(8,128)(2,1)S(1)}, u32[]{:S(2)}, u32[]{:S(2)}) collective-permute-start(bf16[256,2048]{1,0:T(8,128)(2,1)S(1)} %get-tuple-element.7), channel_id=1, source_target_pairs={{0,1},{1,0},{2,3},{3,2},{4,5},{5,4},{6,7},{7,6},{8,9},{9,8},{10,11... | collective-permute-start | bytes 3145736 | tf_op jit(solution)/shard_map/ppermute | solution.py:22
  233.5 75.6 %copy-start.6 = (f32[2048]{0:T(1024)S(1)}, f32[2048]{0:T(1024)}, u32[]{:S(2)}) copy-start(f32[2048]{0:T(1024)} %param.26) | copy-start | bytes 24580
  233.5 25.3 %collective-permute-start.11 = (bf16[256,2048]{1,0:T(8,128)(2,1)S(1)}, bf16[256,2048]{1,0:T(8,128)(2,1)S(1)}, u32[]{:S(2)}, u32[]{:S(2)}) collective-permute-start(bf16[256,2048]{1,0:T(8,128)(2,1)S(1)} %add_convert_fusion.3), channel_id=1, source_target_pairs={{0,2},{1,3},{2,0},{3,1},{4,6},{5,7},{6,4},{7,5},{8,10},{9,11},{10,... | collective-permute-start | bytes 3145736 | tf_op jit(solution)/shard_map/ppermute | solution.py:22
  259.3 53.3 %copy-start.1 = (bf16[1280,1280]{1,0:T(8,128)(2,1)S(1)}, bf16[1280,1280]{1,0:T(8,128)(2,1)}, u32[]{:S(2)}) copy-start(bf16[1280,1280]{1,0:T(8,128)(2,1)} %param.23) | copy-start | bytes 9830404
  260.4 30.0 %all-to-all-start.1 = ((bf16[4,4,16,2048]{3,2,1,0:T(8,128)(2,1)}), bf16[4,4,16,2048]{3,2,1,0:T(8,128)(2,1)}, u32[]{:S(2)}, u32[]{:S(2)}) async-start(bf16[4,4,16,2048]{3,2,1,0:T(8,128)(2,1)} %bitcast.88), calls=%async_computation.1 | async-start | bytes 2097152 | tf_op jit(solution)/shard_map/all_to_all | solution.py:155
  290.3 18.8 %all-to-all-start.2 = ((bf16[4,64,2048]{2,1,0:T(8,128)(2,1)}), bf16[4,64,2048]{2,1,0:T(8,128)(2,1)}, u32[]{:S(2)}, u32[]{:S(2)}) async-start(bf16[4,64,2048]{2,1,0:T(8,128)(2,1)} %bitcast.24), calls=%async_computation.2 | async-start | bytes 2097152 | tf_op jit(solution)/shard_map/all_to_all | solution.py:159
Sparse Core Ops, SparseCore 0:
  108.3 102.5 all-reduce.1
